TPU v7x, 512 devices: a whole 4x8x8 slice. The times are simulated.
512 devices in a mesh: head: 8 (over y), blk: 64 (over z, x, core).
Axes of the slice: x: 4, y: 8, z: 8, core: 2. Of those that a mesh axis runs over, the one named last changes fastest.
Arguments:
- residual: bfloat16 [12288, 2048], P('blk'), may hold values from -100 to 100
- lengths: int32 [64, 6], P('blk'), may hold values from 1 to 96, 192 in all within a row
- token_adapter_index: int32 [12288, 1], P('blk'), may hold values from 0 to 63; in each aligned block of 192 rows (0 to 191, 192 to 383, ...) at most 6 rows name the same one
- attention_norm_gain: float32 [2048], replicated, may hold values from 0.1 to 1.9
- query_key_weight: bfloat16 [2048, 4096], P('blk', 'head'), may hold values from -8 to 8
- value_weight: bfloat16 [2048, 2048], P('blk', 'head'), may hold values from -0.125 to 0.125
- head_second_weight: float32 [8], P('head'), may hold values from 0.2 to 0.8
- output_weight: bfloat16 [2048, 2048], P('blk', 'head'), may hold values from -0.125 to 0.125
- adapter_down_maps: bfloat16 [64, 2048, 16], P('blk', 'head'), may hold values from -0.125 to 0.125
- adapter_up_maps: bfloat16 [64, 16, 2048], P('blk'), may hold values from -1.5 to 1.5
- feedforward_norm_gain: float32 [2048], replicated, may hold values from 0.1 to 1.9
- gate_weight: bfloat16 [2048, 5632], P('blk', 'head'), may hold values from -0.125 to 0.125
- up_weight: bfloat16 [2048, 5632], P('blk', 'head'), may hold values from -0.125 to 0.125
- down_weight: bfloat16 [2048, 5632], P('blk', 'head'), may hold values from -0.078125 to 0.078125
Outputs:
- layer_out: bfloat16 [12288, 2048], P('blk', 'head')
Inputs may be any that keep to these rules, and one draw needn't show every extreme that they name: `lengths`: each row sums to 192, and its largest entry is 96. `token_adapter_index`: among the 192 tokens of one block no adapter is named more than 6 times, a bound that some block reaches.
All inputs are finite; a program needn't handle non-finite values.
Results may differ from a plain program's by a relative error of at most 0.011.
Values may be sent and summed in bfloat16 or wider, within the bound.
No kernel may reach another device: no remote copies, remote signals or barrier semaphores. Data moves between devices by JAX's collectives and lax.ppermute only.
A program may use at most 64 MiB of HBM per device.

v0:
```python
import jax
import jax.numpy as jnp
from jax import lax
from jax.sharding import PartitionSpec as P

HD = 128
adapter_scaling = 2.0
head_shrink = 0.8
neg_large = -1e30


def rms_scale(values, epsilon):
    return values * lax.rsqrt(jnp.mean(values * values, axis=-1, keepdims=True) + epsilon)


def masked_softmax(scores, allowed):
    scores = jnp.where(allowed, scores, neg_large)
    row_peak = jnp.max(scores, axis=-1, keepdims=True)
    raised = jnp.where(allowed, jnp.exp(scores - row_peak), 0.0)
    return raised / jnp.sum(raised, axis=-1, keepdims=True)


def request_mask(lengths_row, length_total):
    ends_at = jnp.cumsum(lengths_row)
    position = jnp.arange(length_total, dtype=jnp.int32)
    request = jnp.sum((position[:, None] >= ends_at[None, :]).astype(jnp.int32), axis=1)
    return (request[:, None] == request[None, :]) & (position[None, :] <= position[:, None])


def diff_head(qk_head, value_head, allowed, lambda_value):
    score_scale = 1.0 / qk_head.shape[-1] ** 0.5
    first_scores = (
        jnp.dot(qk_head[:, 0], qk_head[:, 2].T, precision=lax.Precision.HIGHEST) * score_scale
    )
    second_scores = (
        jnp.dot(qk_head[:, 1], qk_head[:, 3].T, precision=lax.Precision.HIGHEST) * score_scale
    )
    mixed = (
        masked_softmax(first_scores, allowed)
        - lambda_value * masked_softmax(second_scores, allowed)
    ).astype(jnp.bfloat16)
    attended = jnp.dot(mixed, value_head, preferred_element_type=jnp.float32)
    return (rms_scale(attended, 1e-05) * head_shrink).astype(jnp.bfloat16)


def weight_fold(leading, trailing, combine, initial):
    return combine(
        initial,
        (
            lax.all_gather(leading, "blk", axis=0, tiled=True),
            lax.all_gather(trailing, "blk", axis=0, tiled=True),
        ),
        jnp.int32(0),
    )


def head_total(partial_value):
    return lax.psum_scatter(
        partial_value.astype(jnp.bfloat16), "head", scatter_dimension=1, tiled=True
    ).astype(jnp.float32)


def row_products(source):

    def add_rows(totals, pieces, offset):
        return (
            jnp.dot(source, pieces[0], preferred_element_type=jnp.float32),
            jnp.dot(source, pieces[1], preferred_element_type=jnp.float32),
        )

    return add_rows


def per_device(
    residual,
    lengths,
    token_adapter_index,
    attention_norm_gain,
    query_key_weight,
    value_weight,
    head_second_weight,
    output_weight,
    adapter_down_maps,
    adapter_up_maps,
    feedforward_norm_gain,
    gate_weight,
    up_weight,
    down_weight,
):
    tokens = residual.shape[0]
    width = residual.shape[1]
    owners = lax.axis_size("blk")
    capacity = 2 * tokens // owners
    own_width = width // lax.axis_size("head")
    own_begin = lax.axis_index("head") * own_width
    inputs = residual.astype(jnp.float32)
    normed = (rms_scale(inputs, 1e-06) * attention_norm_gain).astype(jnp.bfloat16)
    qk_start = jnp.zeros((tokens, query_key_weight.shape[1]), jnp.float32)
    value_start = jnp.zeros((tokens, value_weight.shape[1]), jnp.float32)
    qk_local, value_local = weight_fold(
        query_key_weight, value_weight, row_products(normed), (qk_start, value_start)
    )
    qk_head = qk_local.reshape(tokens, 4, HD)
    value_head = value_local.astype(jnp.bfloat16)
    allowed = request_mask(lengths[0], tokens)
    head_out = diff_head(qk_head, value_head, allowed, head_second_weight[0])
    chosen = token_adapter_index[:, 0]
    owner_ids = jnp.arange(owners, dtype=jnp.int32)
    member = (chosen[:, None] == owner_ids[None, :]).astype(jnp.int32)
    earlier = jnp.cumsum(member, axis=0) - member
    within = jnp.sum(earlier * member, axis=1)
    target = chosen * capacity + within
    slot_ids = jnp.arange(owners * capacity, dtype=jnp.int32)
    dispatch = (slot_ids[:, None] == target[None, :]).astype(jnp.bfloat16)
    outgoing = jnp.dot(dispatch, head_out, preferred_element_type=jnp.float32).astype(jnp.bfloat16)
    outgoing = outgoing.reshape(owners, capacity, head_out.shape[1])
    received = lax.all_to_all(outgoing, "blk", split_axis=0, concat_axis=0, tiled=True)
    sources = received.shape[0]
    slot_count = received.shape[1]
    flat_heads_output = received.reshape(sources * slot_count, received.shape[2])
    reduced_rank_part = jnp.dot(
        flat_heads_output, adapter_down_maps[0], preferred_element_type=jnp.float32
    )
    reduced_rank_state = lax.psum(reduced_rank_part, "head").astype(jnp.bfloat16)
    adapter_delta = (
        adapter_scaling
        * jnp.dot(reduced_rank_state, adapter_up_maps[0], preferred_element_type=jnp.float32)
    ).astype(jnp.bfloat16)
    returned = lax.all_to_all(
        adapter_delta.reshape(sources, slot_count, width),
        "blk",
        split_axis=0,
        concat_axis=0,
        tiled=True,
    )
    delta_rows = lax.dot_general(
        dispatch,
        returned.reshape(owners * capacity, returned.shape[2]),
        (((0,), (0,)), ((), ())),
        preferred_element_type=jnp.float32,
    )
    delta_own = lax.dynamic_slice_in_dim(delta_rows, own_begin, own_width, 1)
    unit_count = down_weight.shape[1]

    def place_columns(totals, pieces, offset):
        columns = lax.dot_general(
            head_out, pieces[0], (((1,), (1,)), ((), ())), preferred_element_type=jnp.float32
        )
        return (columns, pieces[1])

    projected_start = jnp.zeros((tokens, width), jnp.float32)
    down_start = jnp.zeros((width, unit_count), jnp.bfloat16)
    projected, down_full = weight_fold(
        output_weight, down_weight, place_columns, (projected_start, down_start)
    )
    own_mid = (
        lax.dynamic_slice_in_dim(inputs, own_begin, own_width, 1)
        + head_total(projected)
        + delta_own
    )
    mid_full = lax.all_gather(own_mid.astype(jnp.bfloat16), "head", axis=1, tiled=True)
    ffn_in = (rms_scale(mid_full.astype(jnp.float32), 1e-06) * feedforward_norm_gain).astype(
        jnp.bfloat16
    )
    gate_start = jnp.zeros((tokens, gate_weight.shape[1]), jnp.float32)
    up_start = jnp.zeros((tokens, up_weight.shape[1]), jnp.float32)
    gate_act, upward = weight_fold(
        gate_weight, up_weight, row_products(ffn_in), (gate_start, up_start)
    )
    hidden_units = (jax.nn.silu(gate_act) * upward).astype(jnp.bfloat16)
    ffn_part = lax.dot_general(
        hidden_units, down_full, (((1,), (1,)), ((), ())), preferred_element_type=jnp.float32
    )
    return (own_mid + head_total(ffn_part)).astype(jnp.bfloat16)


def solution(mesh):
    return jax.shard_map(
        per_device,
        mesh=mesh,
        in_specs=(
            P("blk", None),
            P("blk", None),
            P("blk", None),
            P(),
            P("blk", "head"),
            P("blk", "head"),
            P("head"),
            P("blk", "head"),
            P("blk", "head", None),
            P("blk", None, None),
            P(),
            P("blk", "head"),
            P("blk", "head"),
            P("blk", "head"),
        ),
        out_specs=P("blk", "head"),
        check_vma=False,
    )
```

profile of v0, /device:TPU:2, one launch (start us, length us, event | category | flops | bytes accessed | tf_op | source)
XLA Modules:
  0.0 619.7 jit_solution(7784527970061427897)
XLA Ops:
  6.5 0.0 copy-start
  6.5 0.0 all-gather.7.cloned.1.call-start
  6.5 0.7 all-gather.7.cloned.1.call-update
  7.3 0.0 all-gather.9.cloned.1.call-start
  7.3 0.7 all-gather.9.cloned.1.call-update
  8.0 0.0 all-gather.11.cloned.1.call-start
  8.1 0.7 all-gather.11.cloned.1.call-update
  8.7 0.0 reduce-scatter.3.cloned.1.call-start
  8.8 0.8 reduce-window.18
  9.6 0.1 convert_reduce_fusion
  10.4 1.4 multiply_reduce_fusion
  11.7 86.2 %all-gather.7.cloned.1.call-done = bf16[2048,512]{1,0:T(8,128)(2,1)} async-done(((bf16[32,512]{1,0:T(8,128)(2,1)}), bf16[2048,512]{1,0:T(8,128)(2,1)}) %all-gather.7.cloned.1.call-update) | async-done | bytes 2097168 | tf_op jit(solution)/shard_map/all_gather | solution.py:50
  97.9 2.5 fusion.14
  100.4 0.0 copy-start.1
  100.4 0.0 copy-start.5
  100.4 0.1 reshape.92
  100.6 0.3 fusion.40
  100.8 0.4 fusion.42
  101.2 0.4 fusion.41
  101.6 0.1 fusion.22
  101.7 79.3 %all-gather.9.cloned.1.call-done = bf16[2048,256]{1,0:T(8,128)(2,1)} async-done(((bf16[32,256]{1,0:T(8,128)(2,1)}), bf16[2048,256]{1,0:T(8,128)(2,1)}) %all-gather.9.cloned.1.call-update) | async-done | bytes 1048592 | tf_op jit(solution)/shard_map/all_gather | solution.py:51
  181.0 0.0 copy-done.5
  181.0 2.0 multiply_reduce_fusion.1
  182.9 0.0 copy-start.3
  183.0 81.1 %all-gather.11.cloned.1.call-done = bf16[2048,256]{1,0:T(8,128)(2,1)} async-done(((bf16[32,256]{1,0:T(8,128)(2,1)}), bf16[2048,256]{1,0:T(8,128)(2,1)}) %all-gather.11.cloned.1.call-update) | async-done | bytes 1048592 | tf_op jit(solution)/shard_map/all_gather | solution.py:50
  264.1 2.7 convolution_convert_fusion.1
  266.8 0.0 reduce-scatter.3.cloned.1.call-update
  266.8 0.0 all-gather.13.cloned.1.call-start
  266.9 0.5 all-gather.13.cloned.1.call-update
  267.4 0.0 all-gather.15.cloned.1.call-start
  267.4 0.5 all-gather.15.cloned.1.call-update
  268.0 0.0 all-gather.17.cloned.1.call-start
  268.0 0.7 all-gather.17.cloned.1.call-update
  268.8 0.6 reduce-window.19
  269.4 0.2 slice_reduce_fusion
  269.6 0.1 bitcast_bitcast_fusion
  269.8 0.3 convolution_convert_fusion.2
  270.0 0.1 reshape.95
  270.1 19.7 %all_to_all.10 = bf16[64,6,256]{2,1,0:T(8,128)(2,1)S(1)} all-to-all(bf16[64,6,256]{2,1,0:T(8,128)(2,1)S(1)} %reshape.95), channel_id=1, replica_groups=mesh['head'=8,'blk'=64] {'blk'}, dimensions={0} | all-to-all | bytes 393216 | tf_op jit(solution)/shard_map/all_to_all | solution.py:117
  289.8 0.1 reshape.96
  289.9 0.2 fusion.35
  290.1 29.8 %psum.7 = bf16[384,16]{0,1:T(8,128)(2,1)S(1)} all-reduce(f32[384,16]{0,1:T(8,128)S(1)} %fusion.35), channel_id=1, replica_groups=mesh['head'=8,'blk'=64] {'head'}, use_global_device_ids=true, to_apply=%region_12.13 | all-reduce | flops 6144 | bytes 36864 | tf_op jit(solution)/shard_map/psum | solution.py:124
  319.8 0.0 copy-done
  319.9 0.6 multiply_convert_fusion
  320.4 1.6 reshape.97
  322.0 5.6 all-to-all-start.1
  327.7 0.0 reduce-scatter.5.cloned.1.call-start
  327.7 1.4 convert_element_type.59
  329.1 54.3 %all-to-all-done.1 = bf16[64,6,2048]{2,1,0:T(8,128)(2,1)S(1)} async-done(((bf16[64,6,2048]{2,1,0:T(8,128)(2,1)}), bf16[64,6,2048]{2,1,0:T(8,128)(2,1)S(1)}, u32[]{:S(2)}, u32[]{:S(2)}) %all-to-all-start.1) | async-done | bytes 1572896 | tf_op jit(solution)/shard_map/all_to_all | solution.py:129
  383.4 1.4 reshape.98
  384.8 2.0 fusion.12
  386.9 0.0 copy-start.6
  386.9 0.0 reduce-scatter.3.cloned.1.call-done
  386.9 1.0 fusion.37
  388.0 26.0 %all_gather.24 = bf16[192,2048]{1,0:T(8,128)(2,1)S(1)} all-gather(bf16[192,256]{1,0:T(8,128)(2,1)S(1)} %fusion.37), channel_id=1, replica_groups=mesh['head'=8,'blk'=64] {'head'}, dimensions={1}, use_global_device_ids=true | all-gather | bytes 884736 | tf_op jit(solution)/shard_map/all_gather | solution.py:161
  413.9 0.2 fusion
  414.2 0.0 all-gather.13.cloned.1.call-done
  414.2 2.7 fusion.17
  417.0 64.8 %all-gather.15.cloned.1.call-done = bf16[2048,704]{1,0:T(8,128)(2,1)} async-done(((bf16[32,704]{1,0:T(8,128)(2,1)}), bf16[2048,704]{1,0:T(8,128)(2,1)}) %all-gather.15.cloned.1.call-update) | async-done | bytes 2883600 | tf_op jit(solution)/shard_map/all_gather | solution.py:51
  481.7 85.3 %all-gather.17.cloned.1.call-done = bf16[2048,704]{1,0:T(8,128)(2,1)} async-done(((bf16[32,704]{1,0:T(8,128)(2,1)}), bf16[2048,704]{1,0:T(8,128)(2,1)}) %all-gather.17.cloned.1.call-update) | async-done | bytes 2883600 | tf_op jit(solution)/shard_map/all_gather | solution.py:51
  567.0 5.7 convolution_convert_fusion
  572.7 0.0 reduce-scatter.5.cloned.1.call-update
  572.8 38.4 %reduce-scatter.5.cloned.1.call-done = bf16[192,256]{1,0:T(8,128)(2,1)} async-done(((bf16[192,2048]{1,0:T(8,128)(2,1)}), bf16[192,256]{1,0:T(8,128)(2,1)}) %reduce-scatter.5.cloned.1.call-update) | async-done | bytes 98320 | tf_op jit(solution)/shard_map/reduce_scatter | solution.py:58
  611.2 1.7 add_convert_fusion
  (16 shorter events, 0.1 us)
Async XLA Ops:
  6.5 313.3 %copy-start = (bf16[1,16,2048]{2,1,0:T(8,128)(2,1)S(1)}, bf16[1,16,2048]{2,1,0:T(8,128)(2,1)}, u32[]{:S(2)}) copy-start(bf16[1,16,2048]{2,1,0:T(8,128)(2,1)} %param.23) | copy-start | bytes 196612
  6.5 91.4 %all-gather.7.cloned.1.call-start = ((), (), s32[]{:S(2)}) async-start(), calls=%async_computation.4 | async-start | bytes 2129920 | tf_op jit(solution)/shard_map/all_gather | solution.py:50
  7.3 173.7 %all-gather.9.cloned.1.call-start = ((), (), s32[]{:S(2)}) async-start(), calls=%async_computation.5 | async-start | bytes 1064960 | tf_op jit(solution)/shard_map/all_gather | solution.py:51
  8.0 256.1 %all-gather.11.cloned.1.call-start = ((), (), s32[]{:S(2)}) async-start(), calls=%async_computation.6 | async-start | bytes 1064960 | tf_op jit(solution)/shard_map/all_gather | solution.py:50
  8.7 378.2 %reduce-scatter.3.cloned.1.call-start = ((), (), s32[]{:S(2)}) async-start(), calls=%async_computation.7 | async-start | bytes 884736 | tf_op jit(solution)/shard_map/reduce_scatter | solution.py:58
  100.4 80.6 %copy-start.1 = (bf16[192,2048]{1,0:T(8,128)(2,1)S(1)}, bf16[192,2048]{1,0:T(8,128)(2,1)}, u32[]{:S(2)}) copy-start(bf16[192,2048]{1,0:T(8,128)(2,1)} %param.14) | copy-start | bytes 2359300
  100.4 80.6 %copy-start.5 = (f32[2048]{0:T(1024)S(1)}, f32[2048]{0:T(1024)}, u32[]{:S(2)}) copy-start(f32[2048]{0:T(1024)} %param.17) | copy-start | bytes 24580
  182.9 85.8 %copy-start.3 = (s32[192,1]{0,1:T(1,128)S(1)}, s32[192,1]{0,1:T(1,128)}, u32[]{:S(2)}) copy-start(s32[192,1]{0,1:T(1,128)} %param.16) | copy-start | bytes 2308
  266.8 23.1 %copy-start.4 = (bf16[1,256,16]{1,2,0:T(8,128)(2,1)S(1)}, bf16[1,256,16]{1,2,0:T(8,128)(2,1)}, u32[]{:S(2)}) copy-start(bf16[1,256,16]{1,2,0:T(8,128)(2,1)} %param.22) | copy-start | bytes 24580
  266.8 147.4 %all-gather.13.cloned.1.call-start = ((), (), s32[]{:S(2)}) async-start(), calls=%async_computation.8 | async-start | bytes 3194880 | tf_op jit(solution)/shard_map/all_gather | solution.py:50
  267.4 214.3 %all-gather.15.cloned.1.call-start = ((), (), s32[]{:S(2)}) async-start(), calls=%async_computation.9 | async-start | bytes 3194880 | tf_op jit(solution)/shard_map/all_gather | solution.py:51
  268.0 299.0 %all-gather.17.cloned.1.call-start = ((), (), s32[]{:S(2)}) async-start(), calls=%async_computation.10 | async-start | bytes 3194880 | tf_op jit(solution)/shard_map/all_gather | solution.py:51
  322.0 61.4 %all-to-all-start.1 = ((bf16[64,6,2048]{2,1,0:T(8,128)(2,1)}), bf16[64,6,2048]{2,1,0:T(8,128)(2,1)S(1)}, u32[]{:S(2)}, u32[]{:S(2)}) async-start(bf16[64,6,2048]{2,1,0:T(8,128)(2,1)} %reshape.97), calls=%async_computation.2 | async-start | bytes 4194304 | tf_op jit(solution)/shard_map/all_to_all | solution.py:129
  327.7 283.5 %reduce-scatter.5.cloned.1.call-start = ((), (), s32[]{:S(2)}) async-start(), calls=%async_computation.11 | async-start | bytes 884736 | tf_op jit(solution)/shard_map/reduce_scatter | solution.py:58
  386.9 27.3 %copy-start.6 = (f32[2048]{0:T(1024)S(1)}, f32[2048]{0:T(1024)}, u32[]{:S(2)}) copy-start(f32[2048]{0:T(1024)} %param.24) | copy-start | bytes 24580
  416.9 194.2 %copy-start.2 = (bf16[192,256]{1,0:T(8,128)(2,1)S(1)}, bf16[192,256]{1,0:T(8,128)(2,1)}, u32[]{:S(2)}) copy-start(bf16[192,256]{1,0:T(8,128)(2,1)} %reduce-scatter.3.cloned.1.call-done) | copy-start | bytes 294916
Sparse Core Ops, SparseCore 0:
  10.7 87.1 all-gather.6
  101.3 79.6 all-gather.8
  184.3 79.7 all-gather.10
  266.9 38.3 reduce-scatter.2
  309.0 88.1 all-gather.12
  400.9 80.8 all-gather.14
  485.6 81.3 all-gather.16
  572.9 38.2 reduce-scatter.4
where the time goes:
time: 620 us
  waiting for transfers between devices  493 us (80%)
  blocking collectives  75.5 us (12%)
  matrix products  19.4 us (3%)
  between operations  14.3 us (2%)
  other arithmetic  7.53 us (1%)
    all_gather x3, waiting for transfers between devices, weight_fold(): lax.all_gather(trailing, 'blk', axis=0, tiled=True)  229 us
    all_gather x3, waiting for transfers between devices, weight_fold(): lax.all_gather(leading, 'blk', axis=0, tiled=True)  167 us
    all_to_all x1, waiting for transfers between devices, per_device(): lax.all_to_all(adapter_delta.reshape(sources, slot_count, width), 'blk',...  54.3 us
    reduce_scatter x2, waiting for transfers between devices, head_total(): lax.psum_scatter(partial_value.astype(jnp.bfloat16), 'head', scatter_dime...  38.4 us
    psum x1, blocking collectives, per_device(): lax.psum(reduced_rank_part, 'head').astype(jnp.bfloat16)  29.8 us
    all_gather x1, blocking collectives, per_device(): lax.all_gather(own_mid.astype(jnp.bfloat16), 'head', axis=1, tiled=True)  26 us
    all_to_all x1, blocking collectives, per_device(): lax.all_to_all(outgoing, 'blk', split_axis=0, concat_axis=0, tiled=True)  19.7 us
  transfers between devices with their start and end apart: 9, of which 7 were waited for; matrix products, arithmetic and copies ran while one was open for 3% of the time, Pallas kernels for 0%

commit v1 on v0

--- a/solution.py
+++ b/solution.py
@@ -7,6 +7,11 @@
 adapter_scaling = 2.0
 head_shrink = 0.8
 neg_large = -1e30
+
+
+def all_by_exchange(shard, mesh_axis, dim):
+    sent = jnp.stack([shard] * lax.axis_size(mesh_axis))
+    return jnp.concatenate(lax.all_to_all(sent, mesh_axis, 0, 0), axis=dim)
 
 
 def rms_scale(values, epsilon):
@@ -46,10 +51,7 @@
 def weight_fold(leading, trailing, combine, initial):
     return combine(
         initial,
-        (
-            lax.all_gather(leading, "blk", axis=0, tiled=True),
-            lax.all_gather(trailing, "blk", axis=0, tiled=True),
-        ),
+        (lax.all_gather(leading, "blk", axis=0, tiled=True), all_by_exchange(trailing, "blk", 0)),
         jnp.int32(0),
     )
 

time: 620 us -> 418 us (0.67)
  waiting for transfers between devices: 493 us -> 261 us
  starting transfers between devices: 5.91 us -> 31.8 us
    all_gather x3 -> x0, waiting for transfers between devices: 229 us -> none  [weight_fold(): lax.all_gather(trailing, 'blk', axis=0, tiled=True)]
    all_to_all x0 -> x3, waiting for transfers between devices: none -> 42.2 us  [all_by_exchange(): return jnp.concatenate(lax.all_to_all(sent, mesh_axis, 0, 0), axis=dim)]
    all_to_all x0 -> x3, starting transfers between devices: none -> 26.3 us  [all_by_exchange(): return jnp.concatenate(lax.all_to_all(sent, mesh_axis, 0, 0), axis=dim)]
    all_gather x3, waiting for transfers between devices: 167 us -> 141 us  [weight_fold(): lax.all_gather(leading, 'blk', axis=0, tiled=True)]
    all_to_all x1, waiting for transfers between devices: 54.3 us -> 36.5 us  [per_device(): lax.all_to_all(adapter_delta.reshape(sources, slot_count, width), 'blk',...]
  transfers between devices with their start and end apart: 9 -> 9, of which waited for: 7 -> 6; matrix products, arithmetic and copies ran while one was open for 3% -> 5% of each run, Pallas kernels for 0% -> 0%
where the time goes in v1:
time: 418 us; the launch traced here: 417 us
  waiting for transfers between devices  261 us (62%)
  blocking collectives  76.7 us (18%)
  starting transfers between devices  31.8 us (8%)
  matrix products  17.9 us (4%)
  between operations  14.1 us (3%)
  local copies, waits for them, and re-layouts  9.81 us (2%)
  other arithmetic  5.75 us (1%)
    all_gather x3, waiting for transfers between devices, weight_fold(): lax.all_gather(leading, 'blk', axis=0, tiled=True)  141 us
    all_to_all x3, waiting for transfers between devices, all_by_exchange(): return jnp.concatenate(lax.all_to_all(sent, mesh_axis, 0, 0), axis=dim)  42.2 us
    reduce_scatter x2, waiting for transfers between devices, head_total(): lax.psum_scatter(partial_value.astype(jnp.bfloat16), 'head', scatter_dime...  39.2 us
    all_to_all x1, waiting for transfers between devices, per_device(): lax.all_to_all(adapter_delta.reshape(sources, slot_count, width), 'blk',...  36.5 us
    psum x1, blocking collectives, per_device(): lax.psum(reduced_rank_part, 'head').astype(jnp.bfloat16)  29.8 us
    all_gather x1, blocking collectives, per_device(): lax.all_gather(own_mid.astype(jnp.bfloat16), 'head', axis=1, tiled=True)  27.2 us
    all_to_all x3, starting transfers between devices, all_by_exchange(): return jnp.concatenate(lax.all_to_all(sent, mesh_axis, 0, 0), axis=dim)  26.3 us
    all_to_all x1, blocking collectives, per_device(): lax.all_to_all(outgoing, 'blk', split_axis=0, concat_axis=0, tiled=True)  19.7 us
  transfers between devices with their start and end apart: 9, of which 6 were waited for; matrix products, arithmetic and copies ran while one was open for 5% of the time, Pallas kernels for 0%

profile of v1, /device:TPU:2, one launch (start us, length us, event | category | flops | bytes accessed | tf_op | source)
XLA Modules:
  0.0 417.1 jit_solution(14730130877273883059)
XLA Ops:
  6.5 0.0 copy-start
  6.5 0.0 all-gather.4.cloned.1.call-start
  6.5 0.7 all-gather.4.cloned.1.call-update
  7.3 0.0 copy-start.5
  7.3 1.9 stack.6
  9.2 14.0 %all-to-all-start = ((bf16[64,32,256]{2,1,0:T(8,128)(2,1)}), bf16[64,32,256]{2,1,0:T(8,128)(2,1)S(1)}, u32[]{:S(2)}, u32[]{:S(2)}) async-start(bf16[64,32,256]{2,1,0:T(8,128)(2,1)} %stack.6), calls=%async_computation | async-start | bytes 2097152 | tf_op jit(solution)/shard_map/all_to_all | solution.py:14
  23.2 0.6 reduce-window.19
  23.9 0.2 slice_reduce_fusion
  24.1 0.2 reduce-window.18
  24.9 0.1 convert_reduce_fusion
  25.0 0.1 bitcast_bitcast_fusion
  25.1 0.0 copy-done.1
  25.1 0.2 multiply_reduce_fusion
  25.4 73.9 %all-gather.4.cloned.1.call-done = bf16[2048,512]{1,0:T(8,128)(2,1)} async-done(((bf16[32,512]{1,0:T(8,128)(2,1)}), bf16[2048,512]{1,0:T(8,128)(2,1)}) %all-gather.4.cloned.1.call-update) | async-done | bytes 2097168 | tf_op jit(solution)/shard_map/all_gather | solution.py:54
  99.3 2.2 fusion.14
  101.5 0.1 reshape.107
  101.7 0.3 fusion.40
  102.0 0.4 fusion.41
  102.3 0.4 fusion.42
  102.7 0.1 fusion.22
  102.9 0.0 all-to-all-done
  102.9 0.0 copy-start.3
  102.9 0.7 multiply_reduce_fusion.1
  103.6 0.3 convolution_convert_fusion.2
  103.9 0.1 reshape.111
  104.0 19.7 %all_to_all.25 = bf16[64,6,256]{2,1,0:T(8,128)(2,1)S(1)} all-to-all(bf16[64,6,256]{2,1,0:T(8,128)(2,1)S(1)} %reshape.111), channel_id=1, replica_groups=mesh['head'=8,'blk'=64] {'blk'}, dimensions={0} | all-to-all | bytes 393216 | tf_op jit(solution)/shard_map/all_to_all | solution.py:119
  123.7 2.1 stack.8
  125.8 6.3 %all-to-all-start.4 = ((bf16[64,32,704]{2,1,0:T(8,128)(2,1)}), bf16[64,32,704]{2,1,0:T(8,128)(2,1)}, u32[]{:S(2)}, u32[]{:S(2)}) async-start(bf16[64,32,704]{2,1,0:T(8,128)(2,1)} %stack.8), calls=%async_computation.5 | async-start | bytes 6291456 | tf_op jit(solution)/shard_map/all_to_all | solution.py:14
  132.1 0.0 all-gather.6.cloned.1.call-start
  132.1 0.7 all-gather.6.cloned.1.call-update
  132.8 0.1 reshape.112
  132.9 0.2 fusion.35
  133.0 29.8 %psum.7 = bf16[384,16]{0,1:T(8,128)(2,1)S(1)} all-reduce(f32[384,16]{0,1:T(8,128)S(1)} %fusion.35), channel_id=1, replica_groups=mesh['head'=8,'blk'=64] {'head'}, use_global_device_ids=true, to_apply=%region_12.13 | all-reduce | flops 6144 | bytes 36864 | tf_op jit(solution)/shard_map/psum | solution.py:126
  162.8 0.6 multiply_convert_fusion
  163.4 1.6 reshape.113
  165.0 42.2 %all-to-all-done.4 = bf16[64,32,704]{2,1,0:T(8,128)(2,1)} async-done(((bf16[64,32,704]{2,1,0:T(8,128)(2,1)}), bf16[64,32,704]{2,1,0:T(8,128)(2,1)}, u32[]{:S(2)}, u32[]{:S(2)}) %all-to-all-start.4) | async-done | bytes 2883616 | tf_op jit(solution)/shard_map/all_to_all | solution.py:14
  207.2 5.4 %all-to-all-start.2 = ((bf16[64,6,2048]{2,1,0:T(8,128)(2,1)}), bf16[64,6,2048]{2,1,0:T(8,128)(2,1)S(1)}, u32[]{:S(2)}, u32[]{:S(2)}) async-start(bf16[64,6,2048]{2,1,0:T(8,128)(2,1)} %reshape.113), calls=%async_computation.3 | async-start | bytes 4194304 | tf_op jit(solution)/shard_map/all_to_all | solution.py:131
  212.6 0.0 copy-start.4
  212.6 0.0 reduce-scatter.3.cloned.1.call-start
  212.7 11.4 %all-gather.6.cloned.1.call-done = bf16[2048,256]{1,0:T(8,128)(2,1)} async-done(((bf16[32,256]{1,0:T(8,128)(2,1)}), bf16[2048,256]{1,0:T(8,128)(2,1)}) %all-gather.6.cloned.1.call-update) | async-done | bytes 1048592 | tf_op jit(solution)/shard_map/all_gather | solution.py:54
  224.1 2.6 convolution_convert_fusion.1
  226.7 0.0 reduce-scatter.3.cloned.1.call-update
  226.7 0.0 all-gather.8.cloned.1.call-start
  226.8 0.5 all-gather.8.cloned.1.call-update
  227.3 36.5 %all-to-all-done.2 = bf16[64,6,2048]{2,1,0:T(8,128)(2,1)S(1)} async-done(((bf16[64,6,2048]{2,1,0:T(8,128)(2,1)}), bf16[64,6,2048]{2,1,0:T(8,128)(2,1)S(1)}, u32[]{:S(2)}, u32[]{:S(2)}) %all-to-all-start.2) | async-done | bytes 1572896 | tf_op jit(solution)/shard_map/all_to_all | solution.py:131
  263.8 0.0 copy-done.4
  263.8 2.0 stack.7
  265.8 6.0 %all-to-all-start.3 = ((bf16[64,32,704]{2,1,0:T(8,128)(2,1)}), bf16[64,32,704]{2,1,0:T(8,128)(2,1)}, u32[]{:S(2)}, u32[]{:S(2)}) async-start(bf16[64,32,704]{2,1,0:T(8,128)(2,1)} %stack.7), calls=%async_computation.4 | async-start | bytes 6291456 | tf_op jit(solution)/shard_map/all_to_all | solution.py:14
  271.8 0.0 reduce-scatter.5.cloned.1.call-start
  271.9 1.4 convert_element_type.59
  273.2 1.4 reshape.114
  274.7 2.0 fusion.12
  276.7 0.0 copy-start.8
  276.7 0.0 reduce-scatter.3.cloned.1.call-done
  276.7 1.0 fusion.37
  277.7 27.2 %all_gather.14 = bf16[192,2048]{1,0:T(8,128)(2,1)S(1)} all-gather(bf16[192,256]{1,0:T(8,128)(2,1)S(1)} %fusion.37), channel_id=1, replica_groups=mesh['head'=8,'blk'=64] {'head'}, dimensions={1}, use_global_device_ids=true | all-gather | bytes 884736 | tf_op jit(solution)/shard_map/all_gather | solution.py:163
  305.0 0.2 fusion
  305.2 56.0 %all-gather.8.cloned.1.call-done = bf16[2048,704]{1,0:T(8,128)(2,1)} async-done(((bf16[32,704]{1,0:T(8,128)(2,1)}), bf16[2048,704]{1,0:T(8,128)(2,1)}) %all-gather.8.cloned.1.call-update) | async-done | bytes 2883600 | tf_op jit(solution)/shard_map/all_gather | solution.py:54
  361.2 2.7 fusion.17
  363.9 0.0 all-to-all-done.3
  363.9 5.8 %convolution_convert_fusion = bf16[192,2048]{1,0:T(8,128)(2,1)} fusion(bf16[2048,704]{1,0:T(8,128)(2,1)} %bitcast.13, bf16[2048,704]{1,0:T(8,128)(2,1)} %bitcast.12, f32[192,704]{1,0:T(8,128)S(1)} %fusion.17, bf16[192,2048]{1,0:T(8,128)(2,1)S(1)} %all_gather.14, f32[2048]{0:T(1024)S(1)} %copy-done.8, f32[192]{0:T(256)S(1)} %add_rsqrt_fusion), kind=kOutput, calls=%fused_computation.1 | convolution fusion | flops 1110073344 | bytes 7889664 | tf_op jit(solution)/shard_map/dot_general | solution.py:173
  369.7 0.0 reduce-scatter.5.cloned.1.call-update
  369.8 39.2 %reduce-scatter.5.cloned.1.call-done = bf16[192,256]{1,0:T(8,128)(2,1)} async-done(((bf16[192,2048]{1,0:T(8,128)(2,1)}), bf16[192,256]{1,0:T(8,128)(2,1)}) %reduce-scatter.5.cloned.1.call-update) | async-done | bytes 98320 | tf_op jit(solution)/shard_map/reduce_scatter | solution.py:60
  408.9 1.7 add_convert_fusion
  (22 shorter events, 0.2 us)
Async XLA Ops:
  6.5 156.3 %copy-start = (bf16[1,16,2048]{2,1,0:T(8,128)(2,1)S(1)}, bf16[1,16,2048]{2,1,0:T(8,128)(2,1)}, u32[]{:S(2)}) copy-start(bf16[1,16,2048]{2,1,0:T(8,128)(2,1)} %param.23) | copy-start | bytes 196612
  6.5 92.8 %all-gather.4.cloned.1.call-start = ((), (), s32[]{:S(2)}) async-start(), calls=%async_computation.7 | async-start | bytes 2129920 | tf_op jit(solution)/shard_map/all_gather | solution.py:54
  7.3 15.9 %copy-start.5 = (s32[192,1]{0,1:T(1,128)S(1)}, s32[192,1]{0,1:T(1,128)}, u32[]{:S(2)}) copy-start(s32[192,1]{0,1:T(1,128)} %param.16) | copy-start | bytes 2308
  7.3 16.8 %copy-start.9 = (s32[1,6]{1,0:T(1,128)S(1)}, s32[1,6]{1,0:T(1,128)}, u32[]{:S(2)}) copy-start(s32[1,6]{1,0:T(1,128)} %param.15) | copy-start | bytes 76
  7.3 17.9 %copy-start.1 = (bf16[192,2048]{1,0:T(8,128)(2,1)S(1)}, bf16[192,2048]{1,0:T(8,128)(2,1)}, u32[]{:S(2)}) copy-start(bf16[192,2048]{1,0:T(8,128)(2,1)} %param.14) | copy-start | bytes 2359300
  9.2 90.1 %copy-start.7 = (f32[2048]{0:T(1024)S(1)}, f32[2048]{0:T(1024)}, u32[]{:S(2)}) copy-start(f32[2048]{0:T(1024)} %param.17) | copy-start | bytes 24580
  9.2 93.7 %all-to-all-start = ((bf16[64,32,256]{2,1,0:T(8,128)(2,1)}), bf16[64,32,256]{2,1,0:T(8,128)(2,1)S(1)}, u32[]{:S(2)}, u32[]{:S(2)}) async-start(bf16[64,32,256]{2,1,0:T(8,128)(2,1)} %stack.6), calls=%async_computation | async-start | bytes 2097152 | tf_op jit(solution)/shard_map/all_to_all | solution.py:14
  102.9 20.8 %copy-start.3 = (bf16[32,704]{1,0:T(8,128)(2,1)S(1)}, bf16[32,704]{1,0:T(8,128)(2,1)}, u32[]{:S(2)}) copy-start(bf16[32,704]{1,0:T(8,128)(2,1)} %param.27) | copy-start | bytes 135172
  125.8 7.1 %copy-start.6 = (bf16[1,256,16]{1,2,0:T(8,128)(2,1)S(1)}, bf16[1,256,16]{1,2,0:T(8,128)(2,1)}, u32[]{:S(2)}) copy-start(bf16[1,256,16]{1,2,0:T(8,128)(2,1)} %param.22) | copy-start | bytes 24580
  125.8 81.5 %all-to-all-start.4 = ((bf16[64,32,704]{2,1,0:T(8,128)(2,1)}), bf16[64,32,704]{2,1,0:T(8,128)(2,1)}, u32[]{:S(2)}, u32[]{:S(2)}) async-start(bf16[64,32,704]{2,1,0:T(8,128)(2,1)} %stack.8), calls=%async_computation.5 | async-start | bytes 6291456 | tf_op jit(solution)/shard_map/all_to_all | solution.py:14
  132.1 92.0 %all-gather.6.cloned.1.call-start = ((), (), s32[]{:S(2)}) async-start(), calls=%async_computation.8 | async-start | bytes 1064960 | tf_op jit(solution)/shard_map/all_gather | solution.py:54
  207.2 56.6 %all-to-all-start.2 = ((bf16[64,6,2048]{2,1,0:T(8,128)(2,1)}), bf16[64,6,2048]{2,1,0:T(8,128)(2,1)S(1)}, u32[]{:S(2)}, u32[]{:S(2)}) async-start(bf16[64,6,2048]{2,1,0:T(8,128)(2,1)} %reshape.113), calls=%async_computation.3 | async-start | bytes 4194304 | tf_op jit(solution)/shard_map/all_to_all | solution.py:131
  212.6 51.2 %copy-start.4 = (bf16[32,704]{1,0:T(8,128)(2,1)S(1)}, bf16[32,704]{1,0:T(8,128)(2,1)}, u32[]{:S(2)}) copy-start(bf16[32,704]{1,0:T(8,128)(2,1)} %param.26) | copy-start | bytes 135172
  212.6 64.1 %reduce-scatter.3.cloned.1.call-start = ((), (), s32[]{:S(2)}) async-start(), calls=%async_computation.9 | async-start | bytes 884736 | tf_op jit(solution)/shard_map/reduce_scatter | solution.py:60
  226.7 134.5 %all-gather.8.cloned.1.call-start = ((), (), s32[]{:S(2)}) async-start(), calls=%async_computation.10 | async-start | bytes 3194880 | tf_op jit(solution)/shard_map/all_gather | solution.py:54
  265.8 98.1 %all-to-all-start.3 = ((bf16[64,32,704]{2,1,0:T(8,128)(2,1)}), bf16[64,32,704]{2,1,0:T(8,128)(2,1)}, u32[]{:S(2)}, u32[]{:S(2)}) async-start(bf16[64,32,704]{2,1,0:T(8,128)(2,1)} %stack.7), calls=%async_computation.4 | async-start | bytes 6291456 | tf_op jit(solution)/shard_map/all_to_all | solution.py:14
  271.8 137.1 %reduce-scatter.5.cloned.1.call-start = ((), (), s32[]{:S(2)}) async-start(), calls=%async_computation.11 | async-start | bytes 884736 | tf_op jit(solution)/shard_map/reduce_scatter | solution.py:60
  276.7 84.5 %copy-start.8 = (f32[2048]{0:T(1024)S(1)}, f32[2048]{0:T(1024)}, u32[]{:S(2)}) copy-start(f32[2048]{0:T(1024)} %param.24) | copy-start | bytes 24580
  363.9 45.0 %copy-start.2 = (bf16[192,256]{1,0:T(8,128)(2,1)S(1)}, bf16[192,256]{1,0:T(8,128)(2,1)}, u32[]{:S(2)}) copy-start(bf16[192,256]{1,0:T(8,128)(2,1)} %reduce-scatter.3.cloned.1.call-done) | copy-start | bytes 294916
Sparse Core Ops, SparseCore 0:
  10.7 88.5 all-gather.3
  136.3 87.7 all-gather.5
  226.9 38.9 reduce-scatter.2
  269.7 91.4 all-gather.7
  369.9 39.0 reduce-scatter.4
